TPU v7x, 32 devices: a whole 2x2x4 slice. The times are simulated.
32 devices in a mesh: dp: 8 (over y, x, core), seq: 4 (over z).
Axes of the slice: x: 2, y: 2, z: 4, core: 2. Of those that a mesh axis runs over, the one named last changes fastest.
Arguments:
- image_query: bfloat16 [8, 256, 1536], P('dp', 'seq'), may hold values from -300 to 300
- image_key: bfloat16 [8, 256, 1536], P('dp', 'seq'), may hold values from -300 to 300
- image_value: bfloat16 [8, 256, 1536], P('dp', 'seq'), may hold values from -6 to 6
- text_key: bfloat16 [8, 512, 1536], P('dp', 'seq'), may hold values from -300 to 300
- text_value: bfloat16 [8, 512, 1536], P('dp', 'seq'), may hold values from -6 to 6
- query_gain: float32 [128], replicated, may hold values from 0.6 to 1.8
- key_gain: float32 [128], replicated, may hold values from 0.6 to 1.8
- embed_weight: bfloat16 [1536, 1408], replicated, may hold values from -0.15625 to 0.15625
- position_embed: float32 [64, 1408], replicated, may hold values from -2.7 to 2.7
- norm_gain: float32 [1408], replicated, may hold values from 0.25 to 1.75
- final_gain: float32 [1408], replicated, may hold values from 0.25 to 1.75
- up_weight: bfloat16 [3072, 1408], P(('dp', 'seq')), may hold values from -0.15625 to 0.15625
- down_weight: bfloat16 [3072, 1408], P(('dp', 'seq')), may hold values from -0.109375 to 0.109375
- reward_direction: float32 [1408], replicated, may hold values from -1.5 to 1.5
Outputs:
- attended: bfloat16 [8, 256, 1536], P('dp', None, 'seq')
- attended_gradient: bfloat16 [8, 256, 1536], P('dp', None, 'seq')
- reward: float32 [8], P('dp')
All inputs are finite; a program needn't handle non-finite values.
Results may differ from a plain program's by a relative error of at most 0.02.
Values may be sent and summed in bfloat16 or wider, within the bound.
A program may use at most 64 MiB of HBM per device.

v0:
```python
import math

import jax
import jax.numpy as jnp
from jax import lax
from jax.sharding import PartitionSpec as P

HEAD = 128
PATCH_W = 32


epsilon = 1e-06
root_half = 0.7071067811865476
inv_root_tau = 0.3989422804014327


def norm_heads(features, gain_vector):
    token_count = features.shape[0]
    grouped = features.astype(jnp.float32).reshape(token_count, -1, HEAD)
    inverse_rms = lax.rsqrt(jnp.mean(grouped * grouped, axis=-1, keepdims=True) + epsilon)
    return (grouped * inverse_rms * gain_vector).astype(jnp.bfloat16)


def layer_stats(residual):
    centered = residual - jnp.mean(residual, axis=-1, keepdims=True)
    inverse_std = lax.rsqrt(jnp.mean(centered * centered, axis=-1, keepdims=True) + epsilon)
    return (centered * inverse_std, inverse_std)


def layer_back(upstream, normed, inverse_std):
    return inverse_std * (
        upstream
        - jnp.mean(upstream, axis=-1, keepdims=True)
        - normed * jnp.mean(upstream * normed, axis=-1, keepdims=True)
    )


def gelu_parts(preact):
    cumulative = 0.5 * (1.0 + lax.erf(preact * root_half))
    activation = preact * cumulative
    derivative = cumulative + preact * jnp.exp(-0.5 * preact * preact) * inv_root_tau
    return (activation, derivative)


def pool_patches(attended):
    token_count, feature_width = attended.shape
    patch_grid = attended.astype(jnp.float32).reshape(
        token_count // PATCH_W // 2, 2, PATCH_W // 2, 2, feature_width
    )
    return jnp.mean(patch_grid, axis=(1, 3)).reshape(-1, feature_width).astype(jnp.bfloat16)


def spread_patches(pooled_slope):
    pooled_count, feature_width = pooled_slope.shape
    row_count = pooled_count // (PATCH_W // 2)
    patch_grid = pooled_slope.reshape(row_count, 1, PATCH_W // 2, 1, feature_width)
    patch_grid = jnp.broadcast_to(0.25 * patch_grid, (row_count, 2, PATCH_W // 2, 2, feature_width))
    return patch_grid.reshape(4 * pooled_count, feature_width).astype(jnp.bfloat16)


def contract_rows(left_side, right_side):
    return lax.dot_general(
        left_side, right_side, (((1,), (1,)), ((), ())), preferred_element_type=jnp.float32
    )


def round_term(partial_sum):
    return lax.optimization_barrier(partial_sum.astype(jnp.bfloat16)).astype(jnp.float32)


def attend(queries, key_heads, value_heads):
    query_count = queries.shape[0]
    block_rows = math.gcd(query_count, 512)
    query_blocks = queries.reshape(query_count // block_rows, block_rows, queries.shape[1], HEAD)

    def one_block(query_block):
        scores = jnp.einsum(
            "qhd,khd->hqk", query_block, key_heads, preferred_element_type=jnp.float32
        ) * HEAD ** (-0.5)
        exponent = jnp.exp(scores)
        attention_weights = (exponent / jnp.sum(exponent, axis=-1, keepdims=True)).astype(
            jnp.bfloat16
        )
        mixed_heads = jnp.einsum(
            "hqk,khd->qhd", attention_weights, value_heads, preferred_element_type=jnp.float32
        )
        return mixed_heads.astype(jnp.bfloat16)

    mixed_blocks = lax.map(one_block, query_blocks)
    return mixed_blocks.reshape(query_count, -1)


def on_device(
    image_query,
    image_key,
    image_value,
    text_key,
    text_value,
    query_gain,
    key_gain,
    embed_weight,
    position_embed,
    norm_gain,
    final_gain,
    up_weight,
    down_weight,
    reward_direction,
):
    exchanged = (
        lax.all_to_all(image_query, "seq", split_axis=2, concat_axis=1, tiled=True),
        lax.all_to_all(image_key, "seq", split_axis=2, concat_axis=1, tiled=True),
        lax.all_to_all(image_value, "seq", split_axis=2, concat_axis=1, tiled=True),
        lax.all_to_all(text_key, "seq", split_axis=2, concat_axis=1, tiled=True),
        lax.all_to_all(text_value, "seq", split_axis=2, concat_axis=1, tiled=True),
    )
    queries = norm_heads(exchanged[0][0], query_gain)
    key_heads = norm_heads(jnp.concatenate([exchanged[3][0], exchanged[1][0]], axis=0), key_gain)
    value_rows = jnp.concatenate([exchanged[4][0], exchanged[2][0]], axis=0)
    value_heads = value_rows.reshape(value_rows.shape[0], -1, HEAD)
    attended = attend(queries, key_heads, value_heads)
    pooled = pool_patches(attended)
    group_width = pooled.shape[1]
    embed_rows = lax.dynamic_slice_in_dim(
        embed_weight, lax.axis_index("seq") * group_width, group_width, 0
    )
    residual_in = (
        jnp.dot(
            lax.all_gather(pooled, "seq", axis=1, tiled=True),
            embed_weight,
            preferred_element_type=jnp.float32,
        )
        + position_embed
    )
    normed_in, inverse_in = layer_stats(residual_in)
    hidden_in = (normed_in * norm_gain).astype(jnp.bfloat16)
    gathered_up, gathered_down = (
        lax.all_gather(up_weight, "dp", axis=0, tiled=True),
        lax.all_gather(down_weight, "dp", axis=0, tiled=True),
    )
    activation, derivative = gelu_parts(contract_rows(hidden_in, gathered_up))
    branch = jnp.dot(
        activation.astype(jnp.bfloat16), gathered_down, preferred_element_type=jnp.float32
    )
    residual_out = residual_in + lax.psum(round_term(branch).astype(jnp.bfloat16), "seq").astype(
        jnp.float32
    )
    normed_out, inverse_out = layer_stats(residual_out)
    direction = final_gain * reward_direction
    reward = jnp.mean(jnp.sum(normed_out * direction, axis=-1))
    out_slope = layer_back(direction, normed_out, inverse_out)
    slope_low = out_slope.astype(jnp.bfloat16)
    hidden_slope = (contract_rows(slope_low, gathered_down) * derivative).astype(jnp.bfloat16)
    slope_part = jnp.dot(hidden_slope, gathered_up, preferred_element_type=jnp.float32)
    slope_in = lax.psum(round_term(slope_part).astype(jnp.bfloat16), "seq").astype(jnp.float32)
    input_slope = out_slope + layer_back(slope_in * norm_gain, normed_in, inverse_in)
    pooled_slope = contract_rows(input_slope.astype(jnp.bfloat16), embed_rows)
    return (attended[None], spread_patches(pooled_slope)[None], reward.reshape(1))


def solution(mesh):
    return jax.shard_map(
        on_device,
        mesh=mesh,
        in_specs=(
            P("dp", "seq", None),
            P("dp", "seq", None),
            P("dp", "seq", None),
            P("dp", "seq", None),
            P("dp", "seq", None),
            P(),
            P(),
            P(),
            P(),
            P(),
            P(),
            P(("dp", "seq"), None),
            P(("dp", "seq"), None),
            P(),
        ),
        out_specs=(P("dp", None, "seq"), P("dp", None, "seq"), P("dp")),
        check_vma=False,
    )
```

profile of v0, /device:TPU:0, one launch (start us, length us, event | category | flops | bytes accessed | tf_op | source)
XLA Modules:
  0.0 218.8 jit_solution(16248847005396313269)
XLA Ops:
  7.9 2.0 copy.90
  10.5 8.8 %reduce.3 = bf16[1536,64]{1,0:T(8,128)(2,1)S(1)} reduce(bf16[1536,1,64]{2,1,0:T(2,128)(2,1)S(1)} %bitcast.49, bf16[]{:T(256)} %broadcast.126), dimensions={1}, to_apply=%bitcast.31.reduce_sub_computation | reduce | bytes 393218
  20.3 6.3 %all-to-all-start.2 = ((bf16[4,2,12288]{2,1,0:T(2,128)(2,1)}), bf16[4,2,12288]{2,1,0:T(2,128)(2,1)S(1)}, u32[]{:S(2)}, u32[]{:S(2)}) async-start(bf16[4,2,12288]{2,1,0:T(2,128)(2,1)} %reshape.139), calls=%async_computation.2 | async-start | bytes 393216 | tf_op jit(solution)/shard_map/all_to_all | solution.py:110
  27.2 8.8 %reduce.1 = bf16[1536,64]{1,0:T(8,128)(2,1)S(1)} reduce(bf16[1536,1,64]{2,1,0:T(2,128)(2,1)S(1)} %bitcast.52, bf16[]{:T(256)} %broadcast.126), dimensions={1}, to_apply=%bitcast.27.reduce_sub_computation | reduce | bytes 393218
  37.0 5.1 %all-to-all-start.4 = ((bf16[4,2,12288]{2,1,0:T(2,128)(2,1)}), bf16[4,2,12288]{2,1,0:T(2,128)(2,1)S(1)}, u32[]{:S(2)}, u32[]{:S(2)}) async-start(bf16[4,2,12288]{2,1,0:T(2,128)(2,1)} %reshape.135), calls=%async_computation.4 | async-start | bytes 393216 | tf_op jit(solution)/shard_map/all_to_all | solution.py:111
  42.7 8.8 %reduce.4 = bf16[1536,64]{1,0:T(8,128)(2,1)S(1)} reduce(bf16[1536,1,64]{2,1,0:T(2,128)(2,1)S(1)} %bitcast.53, bf16[]{:T(256)} %broadcast.126), dimensions={1}, to_apply=%bitcast.33.reduce_sub_computation | reduce | bytes 393218
  52.5 5.1 %all-to-all-start.1 = ((bf16[4,2,12288]{2,1,0:T(2,128)(2,1)}), bf16[4,2,12288]{2,1,0:T(2,128)(2,1)S(1)}, u32[]{:S(2)}, u32[]{:S(2)}) async-start(bf16[4,2,12288]{2,1,0:T(2,128)(2,1)} %reshape.141), calls=%async_computation.1 | async-start | bytes 393216 | tf_op jit(solution)/shard_map/all_to_all | solution.py:112
  58.9 8.8 %reduce.2 = bf16[1536,128]{1,0:T(8,128)(2,1)S(1)} reduce(bf16[1536,1,128]{2,1,0:T(2,128)(2,1)S(1)} %bitcast.48, bf16[]{:T(256)} %broadcast.126), dimensions={1}, to_apply=%bitcast.29.reduce_sub_computation | reduce | bytes 786434
  68.6 5.2 %all-to-all-start.3 = ((bf16[4,2,24576]{2,1,0:T(2,128)(2,1)}), bf16[4,2,24576]{2,1,0:T(2,128)(2,1)S(1)}, u32[]{:S(2)}, u32[]{:S(2)}) async-start(bf16[4,2,24576]{2,1,0:T(2,128)(2,1)} %reshape.137), calls=%async_computation.3 | async-start | bytes 786432 | tf_op jit(solution)/shard_map/all_to_all | solution.py:113
  74.4 8.8 %reduce.5 = bf16[1536,128]{1,0:T(8,128)(2,1)S(1)} reduce(bf16[1536,1,128]{2,1,0:T(2,128)(2,1)S(1)} %bitcast.44, bf16[]{:T(256)} %broadcast.126), dimensions={1}, to_apply=%bitcast.35.reduce_sub_computation | reduce | bytes 786434
  90.1 5.1 %all-to-all-start = ((bf16[4,2,24576]{2,1,0:T(2,128)(2,1)}), bf16[4,2,24576]{2,1,0:T(2,128)(2,1)S(1)}, u32[]{:S(2)}, u32[]{:S(2)}) async-start(bf16[4,2,24576]{2,1,0:T(2,128)(2,1)} %reshape.143), calls=%async_computation | async-start | bytes 786432 | tf_op jit(solution)/shard_map/all_to_all | solution.py:114
  96.9 7.7 %all-to-all-done = bf16[4,2,24576]{2,1,0:T(2,128)(2,1)S(1)} async-done(((bf16[4,2,24576]{2,1,0:T(2,128)(2,1)}), bf16[4,2,24576]{2,1,0:T(2,128)(2,1)S(1)}, u32[]{:S(2)}, u32[]{:S(2)}) %all-to-all-start) | async-done | bytes 393248 | tf_op jit(solution)/shard_map/all_to_all | solution.py:114
  108.1 13.9 %all_gather.9 = bf16[64,1536]{1,0:T(8,128)(2,1)S(1)} all-gather(bf16[64,384]{1,0:T(8,128)(2,1)S(1)} %bitcast.60), channel_id=1, replica_groups=mesh['dp'=8,'seq'=4] {'seq'}, dimensions={1}, use_global_device_ids=true | all-gather | bytes 245760 | tf_op jit(solution)/shard_map/all_gather | solution.py:128
  121.9 3.2 %fusion.57 = (f32[64]{0:T(128)S(1)}, f32[64,1408]{1,0:T(8,128)S(1)}) fusion(f32[64,1408]{1,0:T(8,128)S(1)} %copy-done.4, bf16[64,1536]{1,0:T(8,128)(2,1)S(1)} %all_gather.9, bf16[1536,1408]{1,0:T(8,128)(2,1)} %param.21), kind=kOutput, calls=%fused_computation.88 | convolution fusion | flops 277004224 | bytes 5243136 | tf_op jit(solution)/shard_map/dot_general | solution.py:127
  125.5 2.4 %fusion.26 = f32[64,768]{1,0:T(8,128)S(1)} fusion(bf16[768,1408]{1,0:T(8,128)(2,1)} %all-gather.3.cloned.1.call-done, f32[64,1408]{1,0:T(8,128)S(1)} %get-tuple-element.47, f32[1408]{0:T(1024)S(1)} %copy-done.7, f32[64]{0:T(128)S(1)} %add_rsqrt_fusion.3, f32[64]{0:T(128)S(1)} %broadcast_multiply_fusion.4), kind=kOutput, calls=%fused_computation.50 | convolution fusion | flops 138772480 | bytes 2725888 | tf_op jit(solution)/shard_map/dot_general | solution.py:62
  127.9 2.9 %convolution_convert_fusion.1 = bf16[64,1408]{1,0:T(8,128)(2,1)} fusion(bf16[768,1408]{1,0:T(8,128)(2,1)} %all-gather.5.cloned.1.call-done, f32[64,768]{1,0:T(8,128)S(1)} %fusion.26), kind=kOutput, calls=%fused_computation.4 | convolution fusion | flops 138747904 | bytes 2539520 | tf_op jit(solution)/shard_map/dot_general | solution.py:141
  130.9 33.7 %all-reduce.3.cloned.1.call-done = bf16[64,1408]{1,0:T(8,128)(2,1)} async-done(((bf16[64,1408]{1,0:T(8,128)(2,1)}), bf16[64,1408]{1,0:T(8,128)(2,1)}) %all-reduce.3.cloned.1.call-update) | async-done | bytes 180240 | tf_op jit(solution)/shard_map/psum | solution.py:144
  164.6 1.1 fusion.55
  165.7 1.1 multiply_reduce_fusion.2
  166.8 1.7 multiply_reduce_fusion.4
  168.6 3.9 %convolution_convert_fusion = bf16[64,1408]{1,0:T(8,128)(2,1)} fusion(bf16[768,1408]{1,0:T(8,128)(2,1)S(1)} %copy-done, bf16[768,1408]{1,0:T(8,128)(2,1)} %all-gather.5.cloned.1.call-done, f32[64,768]{1,0:T(8,128)S(1)} %fusion.26, f32[64]{0:T(128)S(1)} %broadcast_multiply_fusion.2, f32[1408]{0:T(1024)S(1)} %broadcast_subtract_fusion, ...), kind=kOutput, calls=%fused_computation.3 | convolution fusion | flops 278126592 | bytes 5249280 | tf_op jit(solution)/shard_map/dot_general | solution.py:153
  174.0 33.2 %all-reduce.5.cloned.1.call-done = bf16[64,1408]{1,0:T(8,128)(2,1)} async-done(((bf16[64,1408]{1,0:T(8,128)(2,1)}), bf16[64,1408]{1,0:T(8,128)(2,1)}) %all-reduce.5.cloned.1.call-update) | async-done | bytes 180240 | tf_op jit(solution)/shard_map/psum | solution.py:154
  207.2 1.2 fusion.16
  208.4 1.8 fusion.7
  (93 shorter events, 21.2 us)
Async XLA Ops:
  7.2 19.4 %copy-start.5 = (bf16[1,64,1536]{2,1,0:T(8,128)(2,1)S(1)}, bf16[1,64,1536]{2,1,0:T(8,128)(2,1)}, u32[]{:S(2)}) copy-start(bf16[1,64,1536]{2,1,0:T(8,128)(2,1)} %param.15) | copy-start | bytes 589828
  7.2 118.3 %all-gather.3.cloned.1.call-start = ((), (), s32[]{:S(2)}) async-start(), calls=%async_computation.5 | async-start | bytes 2433024 | tf_op jit(solution)/shard_map/all_gather | solution.py:137
  19.3 22.8 %copy-start.6 = (bf16[1,64,1536]{2,1,0:T(8,128)(2,1)S(1)}, bf16[1,64,1536]{2,1,0:T(8,128)(2,1)}, u32[]{:S(2)}) copy-start(bf16[1,64,1536]{2,1,0:T(8,128)(2,1)} %param.16) | copy-start | bytes 589828
  20.3 16.7 %all-to-all-start.2 = ((bf16[4,2,12288]{2,1,0:T(2,128)(2,1)}), bf16[4,2,12288]{2,1,0:T(2,128)(2,1)S(1)}, u32[]{:S(2)}, u32[]{:S(2)}) async-start(bf16[4,2,12288]{2,1,0:T(2,128)(2,1)} %reshape.139), calls=%async_computation.2 | async-start | bytes 393216 | tf_op jit(solution)/shard_map/all_to_all | solution.py:110
  36.0 22.3 %copy-start.2 = (bf16[1,128,1536]{2,1,0:T(8,128)(2,1)S(1)}, bf16[1,128,1536]{2,1,0:T(8,128)(2,1)}, u32[]{:S(2)}) copy-start(bf16[1,128,1536]{2,1,0:T(8,128)(2,1)} %param.17) | copy-start | bytes 1179652
  37.0 15.5 %all-to-all-start.4 = ((bf16[4,2,12288]{2,1,0:T(2,128)(2,1)}), bf16[4,2,12288]{2,1,0:T(2,128)(2,1)S(1)}, u32[]{:S(2)}, u32[]{:S(2)}) async-start(bf16[4,2,12288]{2,1,0:T(2,128)(2,1)} %reshape.135), calls=%async_computation.4 | async-start | bytes 393216 | tf_op jit(solution)/shard_map/all_to_all | solution.py:111
  52.5 16.1 %all-to-all-start.1 = ((bf16[4,2,12288]{2,1,0:T(2,128)(2,1)}), bf16[4,2,12288]{2,1,0:T(2,128)(2,1)S(1)}, u32[]{:S(2)}, u32[]{:S(2)}) async-start(bf16[4,2,12288]{2,1,0:T(2,128)(2,1)} %reshape.141), calls=%async_computation.1 | async-start | bytes 393216 | tf_op jit(solution)/shard_map/all_to_all | solution.py:112
  57.6 16.2 %copy-start.3 = (bf16[1,128,1536]{2,1,0:T(8,128)(2,1)S(1)}, bf16[1,128,1536]{2,1,0:T(8,128)(2,1)}, u32[]{:S(2)}) copy-start(bf16[1,128,1536]{2,1,0:T(8,128)(2,1)} %param.18) | copy-start | bytes 1179652
  57.6 70.3 %all-gather.5.cloned.1.call-start = ((), (), s32[]{:S(2)}) async-start(), calls=%async_computation.6 | async-start | bytes 2433024 | tf_op jit(solution)/shard_map/all_gather | solution.py:138
  68.6 15.5 %copy-start.8 = (f32[1408]{0:T(1024)S(1)}, f32[1408]{0:T(1024)}, u32[]{:S(2)}) copy-start(f32[1408]{0:T(1024)} %param.24) | copy-start | bytes 16900
  68.6 15.5 %copy-start.9 = (f32[1408]{0:T(1024)S(1)}, f32[1408]{0:T(1024)}, u32[]{:S(2)}) copy-start(f32[1408]{0:T(1024)} %param.27) | copy-start | bytes 16900
  68.6 21.5 %all-to-all-start.3 = ((bf16[4,2,24576]{2,1,0:T(2,128)(2,1)}), bf16[4,2,24576]{2,1,0:T(2,128)(2,1)S(1)}, u32[]{:S(2)}, u32[]{:S(2)}) async-start(bf16[4,2,24576]{2,1,0:T(2,128)(2,1)} %reshape.137), calls=%async_computation.3 | async-start | bytes 786432 | tf_op jit(solution)/shard_map/all_to_all | solution.py:113
  89.0 6.6 %copy-start.10 = (f32[128]{0:T(128)S(1)}, f32[128]{0:T(128)}, u32[]{:S(2)}) copy-start(f32[128]{0:T(128)} %param.19) | copy-start | bytes 1540
  90.1 14.5 %all-to-all-start = ((bf16[4,2,24576]{2,1,0:T(2,128)(2,1)}), bf16[4,2,24576]{2,1,0:T(2,128)(2,1)S(1)}, u32[]{:S(2)}, u32[]{:S(2)}) async-start(bf16[4,2,24576]{2,1,0:T(2,128)(2,1)} %reshape.143), calls=%async_computation | async-start | bytes 786432 | tf_op jit(solution)/shard_map/all_to_all | solution.py:114
  95.2 69.4 %all-reduce.3.cloned.1.call-start = ((), (), s32[]{:S(2)}) async-start(), calls=%async_computation.7 | async-start | bytes 360448 | tf_op jit(solution)/shard_map/psum | solution.py:144
  96.9 8.8 %copy-start.11 = (f32[128]{0:T(128)S(1)}, f32[128]{0:T(128)}, u32[]{:S(2)}) copy-start(f32[128]{0:T(128)} %param.20) | copy-start | bytes 1540
  107.2 14.8 %copy-start.4 = (f32[64,1408]{1,0:T(8,128)S(1)}, f32[64,1408]{1,0:T(8,128)}, u32[]{:S(2)}) copy-start(f32[64,1408]{1,0:T(8,128)} %param.22) | copy-start | bytes 1081348
  121.9 3.5 %copy-start.7 = (f32[1408]{0:T(1024)S(1)}, f32[1408]{0:T(1024)}, u32[]{:S(2)}) copy-start(f32[1408]{0:T(1024)} %param.23) | copy-start | bytes 16900
  127.8 40.7 %copy-start = (bf16[768,1408]{1,0:T(8,128)(2,1)S(1)}, bf16[768,1408]{1,0:T(8,128)(2,1)}, u32[]{:S(2)}) copy-start(bf16[768,1408]{1,0:T(8,128)(2,1)} %all-gather.3.cloned.1.call-done) | copy-start | bytes 6488068
  130.8 76.4 %all-reduce.5.cloned.1.call-start = ((), (), s32[]{:S(2)}) async-start(), calls=%async_computation.8 | async-start | bytes 360448 | tf_op jit(solution)/shard_map/psum | solution.py:154
  168.6 39.8 %copy-start.1 = (bf16[64,1408]{1,0:T(8,128)(2,1)S(1)}, bf16[64,1408]{1,0:T(8,128)(2,1)}, u32[]{:S(2)}) copy-start(bf16[64,1408]{1,0:T(8,128)(2,1)} %all-reduce.3.cloned.1.call-done) | copy-start | bytes 540676
Sparse Core Ops, SparseCore 0:
  9.9 30.8 all-gather.2
  60.3 29.6 all-gather.4
  130.9 33.6 all-reduce.2
  172.6 34.5 all-reduce.4
where the time goes:
time: 220 us; the launch traced here: 219 us
  waiting for transfers between devices  76.2 us (35%)
  other arithmetic  52 us (24%)
  starting transfers between devices  26.9 us (12%)
  local copies, waits for them, and re-layouts  17.4 us (8%)
  between operations  16.7 us (8%)
  matrix products  15.7 us (7%)
  blocking collectives  13.9 us (6%)
    unnamed x5, other arithmetic  44.1 us
    psum x1, waiting for transfers between devices, on_device(): lax.psum(round_term(branch).astype(jnp.bfloat16), 'seq').astype(jnp.float32)  33.7 us
    psum x1, waiting for transfers between devices, on_device(): lax.psum(round_term(slope_part).astype(jnp.bfloat16), 'seq')  33.2 us
    all_gather x1, blocking collectives, on_device(): lax.all_gather(pooled, 'seq', axis=1, tiled=True)  13.9 us
    unnamed x43, local copies, waits for them, and re-layouts  12.5 us
    all_to_all x1, waiting for transfers between devices, on_device(): lax.all_to_all(text_value, 'seq', split_axis=2, concat_axis=1, tiled=True)  7.72 us
    all_to_all x1, starting transfers between devices, on_device(): lax.all_to_all(image_query, 'seq', split_axis=2, concat_axis=1, tiled=True)  6.32 us
    all_to_all x1, starting transfers between devices, on_device(): lax.all_to_all(text_key, 'seq', split_axis=2, concat_axis=1, tiled=True)  5.22 us
  transfers between devices with their start and end apart: 9, of which 3 were waited for; matrix products, arithmetic and copies ran while one was open for 32% of the time, Pallas kernels for 0%

commit v1 on v0

v1 whole, which is shorter than its diff:
```python
import functools

import jax
import jax.numpy as jnp
from jax import lax
from jax.experimental import pallas as pl
from jax.experimental.pallas import tpu as pltpu
from jax.sharding import PartitionSpec as P

HEAD = 128
PATCH_W = 32
EPS = 1e-06
ROOT_HALF = 0.7071067811865476
INV_ROOT_TAU = 0.3989422804014327
MESH = pl.DeviceIdType.MESH
F32 = jnp.float32
BF16 = jnp.bfloat16


def norm_head(features, gain):
    wide = features.astype(F32)
    inverse_rms = lax.rsqrt(jnp.mean(wide * wide, axis=-1, keepdims=True) + EPS)
    return (wide * inverse_rms * gain).astype(BF16)


def layer_stats(residual):
    centered = residual - jnp.mean(residual, axis=-1, keepdims=True)
    inverse_std = lax.rsqrt(jnp.mean(centered * centered, axis=-1, keepdims=True) + EPS)
    return centered * inverse_std, inverse_std


def layer_back(upstream, normed, inverse_std):
    return inverse_std * (
        upstream
        - jnp.mean(upstream, axis=-1, keepdims=True)
        - normed * jnp.mean(upstream * normed, axis=-1, keepdims=True)
    )


def gelu_parts(preact):
    cumulative = 0.5 * (1.0 + lax.erf(preact * ROOT_HALF))
    derivative = cumulative + preact * jnp.exp(-0.5 * preact * preact) * INV_ROOT_TAU
    return preact * cumulative, derivative


def dot(left, right):
    return jnp.dot(left, right, preferred_element_type=F32)


def dot_rows(left, right):
    return lax.dot_general(left, right, (((1,), (1,)), ((), ())), preferred_element_type=F32)


def tower_kernel(
    n_dp,
    n_seq,
    gather_here,
    iq_ref,
    ik_ref,
    iv_ref,
    tk_ref,
    tv_ref,
    q_gain_ref,
    k_gain_ref,
    embed_hbm,
    pos_ref,
    norm_gain_ref,
    final_gain_ref,
    up_hbm,
    down_hbm,
    direction_ref,
    attended_ref,
    gradient_ref,
    reward_ref,
    q_buf,
    k_buf,
    v_buf,
    embed,
    up_all,
    down_all,
    pooled_buf,
    resid_in,
    part_buf,
    part_in,
    slope_all,
    part2_buf,
    part2_in,
    slope2_all,
    score_buf,
    local_sem,
    a2a_send,
    a2a_recv,
    w_send,
    w_recv,
    f_send,
    f_recv,
    x_send,
    x_recv,
    s_send,
    s_recv,
):
    dp = lax.axis_index("dp")
    seq = lax.axis_index("seq")
    width = q_buf.shape[2]
    heads = width // HEAD
    img = iq_ref.shape[1]
    txt = tk_ref.shape[1]
    shard = up_hbm.shape[0]
    tokens = resid_in.shape[0]
    mine = tokens // n_seq
    n_chip = n_dp // 2
    core = lax.rem(dp, 2)
    chip = lax.div(dp, 2)

    def peer(d):
        return lax.rem(seq + d, n_seq)

    def source(d):
        return lax.rem(seq + n_seq - d, n_seq)

    def chip_at(d):
        return lax.rem(chip + d, n_chip) * 2 + core

    def chip_from(d):
        return lax.rem(chip + n_chip - d, n_chip) * 2 + core

    sibling = chip * 2 + 1 - core

    def columns(owner):
        return pl.ds(pl.multiple_of(owner * width, HEAD), width)

    def rows(owner, count):
        return pl.ds(pl.multiple_of(owner * count, 16), count)

    def pieces(owner, slot):
        cols = columns(owner)
        return (
            (iq_ref.at[0, :, cols], q_buf.at[slot]),
            (tk_ref.at[0, :, cols], k_buf.at[slot, pl.ds(0, txt)]),
            (ik_ref.at[0, :, cols], k_buf.at[slot, pl.ds(txt, img)]),
            (tv_ref.at[0, :, cols], v_buf.at[slot, pl.ds(0, txt)]),
            (iv_ref.at[0, :, cols], v_buf.at[slot, pl.ds(txt, img)]),
        )

    own_loads = []
    for index, (src, dst) in enumerate(pieces(seq, 0)):
        own_loads.append(pltpu.make_async_copy(src, dst, local_sem.at[index]))
    own_rows = rows(dp, shard) if gather_here else pl.ds(0, shard)
    late_loads = [
        pltpu.make_async_copy(embed_hbm, embed, local_sem.at[5]),
        pltpu.make_async_copy(up_hbm, up_all.at[own_rows], local_sem.at[6]),
        pltpu.make_async_copy(down_hbm, down_all.at[own_rows], local_sem.at[7]),
    ]
    for load in own_loads:
        load.start()

    barrier = pltpu.get_barrier_semaphore()
    partners = 0
    for d in range(1, n_seq):
        pl.semaphore_signal(barrier, inc=1, device_id=(dp, peer(d)), device_id_type=MESH)
        partners += 1
    if gather_here:
        for d in range(1, n_chip):
            pl.semaphore_signal(barrier, inc=1, device_id=(chip_at(d), seq), device_id_type=MESH)
            partners += 1
        pl.semaphore_signal(barrier, inc=1, device_id=(sibling, seq), device_id_type=MESH)
        partners += 1
    pl.semaphore_wait(barrier, partners)

    a2a = {}
    for d in range(1, n_seq):
        for index, (src, dst) in enumerate(pieces(peer(d), d)):
            a2a[d, index] = pltpu.make_async_remote_copy(
                src_ref=src,
                dst_ref=dst,
                send_sem=a2a_send.at[d, index],
                recv_sem=a2a_recv.at[d, index],
                device_id=(dp, peer(d)),
                device_id_type=MESH,
            )
    for index in range(5):
        for d in range(1, n_seq):
            a2a[d, index].start()

    weights, forwards = {}, {}
    if gather_here:
        for index, (src, dst) in enumerate(((up_hbm, up_all), (down_hbm, down_all))):
            for d in range(1, n_chip):
                weights[d, index] = pltpu.make_async_remote_copy(
                    src_ref=src,
                    dst_ref=dst.at[rows(dp, shard)],
                    send_sem=w_send.at[d, index],
                    recv_sem=w_recv.at[d, index],
                    device_id=(chip_at(d), seq),
                    device_id_type=MESH,
                )
                weights[d, index].start()
            for d in range(n_chip):
                held = rows(chip_from(d), shard)
                forwards[d, index] = pltpu.make_async_remote_copy(
                    src_ref=src if d == 0 else dst.at[held],
                    dst_ref=dst.at[held],
                    send_sem=f_send.at[d, index],
                    recv_sem=f_recv.at[d, index],
                    device_id=(sibling, seq),
                    device_id_type=MESH,
                )
            forwards[0, index].start()
    for load in late_loads:
        load.start()
    for load in own_loads:
        load.wait()
    for d in range(1, n_seq):
        a2a[d, 0].wait_recv()

    q_gain = q_gain_ref[...]
    k_gain = k_gain_ref[...]
    queries = []
    for h in range(heads):
        lanes = slice(h * HEAD, (h + 1) * HEAD)
        queries.append(
            jnp.concatenate([norm_head(q_buf[d, :, lanes], q_gain) for d in range(n_seq)], axis=0)
        )
    mixed = [None] * heads
    total = [None] * heads
    for d in range(n_seq):
        if d:
            for index in range(1, 5):
                a2a[d, index].wait_recv()
        for h in range(heads):
            lanes = slice(h * HEAD, (h + 1) * HEAD)
            keys = norm_head(k_buf[d, :, lanes], k_gain)
            exponent = jnp.exp(dot_rows(queries[h], keys) * HEAD**-0.5)
            part_total = jnp.sum(exponent, axis=-1, keepdims=True)
            part_mixed = dot(exponent.astype(BF16), v_buf[d, :, lanes])
            total[h] = part_total if d == 0 else total[h] + part_total
            mixed[h] = part_mixed if d == 0 else mixed[h] + part_mixed
    for h in range(heads):
        lanes = slice(h * HEAD, (h + 1) * HEAD)
        done = (mixed[h] / total[h]).astype(BF16)
        for d in range(n_seq):
            attended_ref[rows(source(d), img), lanes] = done[d * img : (d + 1) * img]

    def pool_map(shape, token_axis):
        token = lax.broadcasted_iota(jnp.int32, shape, token_axis)
        pool = lax.broadcasted_iota(jnp.int32, shape, 1 - token_axis)
        place = lax.div(token, 2 * PATCH_W) * (PATCH_W // 2) + lax.div(lax.rem(token, PATCH_W), 2)
        return jnp.where(place == pool, 0.25, 0.0).astype(BF16)

    image_tokens = attended_ref.shape[0]
    pooled = dot(pool_map((tokens, image_tokens), 1), attended_ref[...])
    pooled_buf[0] = pooled.astype(BF16)

    def spread_to(kind, src_of, dst_of):
        copies = {}
        for d in range(1, n_seq):
            copies[d] = pltpu.make_async_remote_copy(
                src_ref=src_of(d),
                dst_ref=dst_of(d),
                send_sem=x_send.at[kind, d],
                recv_sem=x_recv.at[kind, d],
                device_id=(dp, peer(d)),
                device_id_type=MESH,
            )
            copies[d].start()
        return copies

    pooled_copies = spread_to(0, lambda d: pooled_buf.at[0], lambda d: pooled_buf.at[d])
    for load in late_loads:
        load.wait()
    if gather_here:
        for index in range(2):
            for d in range(1, n_chip):
                weights[d, index].wait_recv()
                forwards[d, index].start()

    residual = pos_ref[...]
    for d in range(n_seq):
        if d:
            pooled_copies[d].wait_recv()
        residual = residual + dot(pooled_buf[d], embed[rows(source(d), width), :])
    resid_in[...] = residual
    normed_in, _ = layer_stats(residual)
    norm_gain = norm_gain_ref[...]
    hidden_in = (normed_in * norm_gain).astype(BF16)
    if gather_here:
        for d in range(n_chip):
            forwards[d, 0].wait_recv()
    activation, derivative = gelu_parts(dot_rows(hidden_in, up_all[...]))
    if gather_here:
        for d in range(n_chip):
            forwards[d, 1].wait_recv()
    part_buf[...] = dot(activation.astype(BF16), down_all[...]).astype(BF16)
    part_copies = spread_to(
        1, lambda d: part_buf.at[rows(peer(d), mine)], lambda d: part_in.at[d]
    )
    own_resid = resid_in[rows(seq, mine), :]
    normed_own, inverse_own = layer_stats(own_resid)
    branch = part_buf[rows(seq, mine), :].astype(F32)
    for d in range(1, n_seq):
        part_copies[d].wait_recv()
        branch = branch + part_in[d].astype(F32)
    normed_out, inverse_out = layer_stats(own_resid + branch)
    direction = final_gain_ref[...] * direction_ref[...]
    out_slope = layer_back(direction, normed_out, inverse_out)
    slope_all[rows(seq, mine), :] = out_slope.astype(BF16)
    own_tokens = rows(seq, mine)
    slope_copies = spread_to(
        2, lambda d: slope_all.at[own_tokens], lambda d: slope_all.at[own_tokens]
    )
    score = jnp.sum(jnp.sum(normed_out * direction, axis=-1, keepdims=True), axis=0, keepdims=True)
    score_buf[0] = jnp.broadcast_to(score, score_buf.shape[1:])
    score_copies = {}
    for d in range(1, n_seq):
        score_copies[d] = pltpu.make_async_remote_copy(
            src_ref=score_buf.at[0],
            dst_ref=score_buf.at[d],
            send_sem=s_send.at[d],
            recv_sem=s_recv.at[d],
            device_id=(dp, peer(d)),
            device_id_type=MESH,
        )
        score_copies[d].start()

    for d in range(1, n_seq):
        slope_copies[d].wait_recv()
    back = dot_rows(slope_all[...], down_all[...])
    part2_buf[...] = dot((back * derivative).astype(BF16), up_all[...]).astype(BF16)
    part2_copies = spread_to(
        3, lambda d: part2_buf.at[rows(peer(d), mine)], lambda d: part2_in.at[d]
    )
    slope_in = part2_buf[rows(seq, mine), :].astype(F32)
    for d in range(1, n_seq):
        part2_copies[d].wait_recv()
        slope_in = slope_in + part2_in[d].astype(F32)
    input_slope = out_slope + layer_back(slope_in * norm_gain, normed_own, inverse_own)
    slope2_all[rows(seq, mine), :] = input_slope.astype(BF16)
    slope2_copies = spread_to(
        4, lambda d: slope2_all.at[own_tokens], lambda d: slope2_all.at[own_tokens]
    )
    score_sum = score_buf[0]
    for d in range(1, n_seq):
        score_copies[d].wait_recv()
        score_sum = score_sum + score_buf[d]
    reward_ref[...] = score_sum * (1.0 / tokens)
    for d in range(1, n_seq):
        slope2_copies[d].wait_recv()
    pooled_slope = dot_rows(slope2_all[...], embed[rows(seq, width), :]).astype(BF16)
    gradient_ref[...] = dot(pool_map((image_tokens, tokens), 0), pooled_slope).astype(BF16)

    for group in (
        a2a,
        weights,
        forwards,
        pooled_copies,
        part_copies,
        slope_copies,
        score_copies,
        part2_copies,
        slope2_copies,
    ):
        for copy in group.values():
            copy.wait_send()


def on_device(
    n_dp,
    n_seq,
    image_query,
    image_key,
    image_value,
    text_key,
    text_value,
    query_gain,
    key_gain,
    embed_weight,
    position_embed,
    norm_gain,
    final_gain,
    up_weight,
    down_weight,
    reward_direction,
):
    gather_here = n_dp % 2 == 0 and n_dp <= 16 and up_weight.shape[0] % 16 == 0
    if not gather_here:
        up_weight = lax.all_gather(up_weight, "dp", axis=0, tiled=True)
        down_weight = lax.all_gather(down_weight, "dp", axis=0, tiled=True)
    img, txt = image_query.shape[1], text_key.shape[1]
    features, emb = embed_weight.shape
    width = features // n_seq
    tokens = position_embed.shape[0]
    mine = tokens // n_seq
    hidden = up_weight.shape[0] * (n_dp if gather_here else 1)
    n_chip = n_dp // 2 if gather_here else 1
    keys = img + txt
    vmem = pl.BlockSpec(memory_space=pltpu.VMEM)
    anywhere = pl.BlockSpec(memory_space=pl.ANY)
    dma = pltpu.SemaphoreType.DMA
    attended, gradient, reward = pl.pallas_call(
        functools.partial(tower_kernel, n_dp, n_seq, gather_here),
        out_shape=(
            jax.ShapeDtypeStruct((img * n_seq, width), BF16),
            jax.ShapeDtypeStruct((img * n_seq, width), BF16),
            jax.ShapeDtypeStruct((8, 128), F32),
        ),
        in_specs=[anywhere] * 5
        + [vmem] * 2
        + [anywhere]
        + [vmem] * 3
        + [anywhere] * 2
        + [vmem],
        out_specs=(vmem, vmem, vmem),
        scratch_shapes=[
            pltpu.VMEM((n_seq, img, width), BF16),
            pltpu.VMEM((n_seq, keys, width), BF16),
            pltpu.VMEM((n_seq, keys, width), BF16),
            pltpu.VMEM((features, emb), BF16),
            pltpu.VMEM((hidden, emb), BF16),
            pltpu.VMEM((hidden, emb), BF16),
            pltpu.VMEM((n_seq, tokens, width), BF16),
            pltpu.VMEM((tokens, emb), F32),
            pltpu.VMEM((tokens, emb), BF16),
            pltpu.VMEM((n_seq, mine, emb), BF16),
            pltpu.VMEM((tokens, emb), BF16),
            pltpu.VMEM((tokens, emb), BF16),
            pltpu.VMEM((n_seq, mine, emb), BF16),
            pltpu.VMEM((tokens, emb), BF16),
            pltpu.VMEM((n_seq, 8, 128), F32),
            dma((8,)),
            dma((n_seq, 5)),
            dma((n_seq, 5)),
            dma((n_chip, 2)),
            dma((n_chip, 2)),
            dma((n_chip, 2)),
            dma((n_chip, 2)),
            dma((5, n_seq)),
            dma((5, n_seq)),
            dma((n_seq,)),
            dma((n_seq,)),
        ],
        compiler_params=pltpu.CompilerParams(
            collective_id=0, has_side_effects=True, vmem_limit_bytes=40 * 1024 * 1024
        ),
    )(
        image_query,
        image_key,
        image_value,
        text_key,
        text_value,
        query_gain.reshape(1, -1),
        key_gain.reshape(1, -1),
        embed_weight,
        position_embed,
        norm_gain.reshape(1, -1),
        final_gain.reshape(1, -1),
        up_weight,
        down_weight,
        reward_direction.reshape(1, -1),
    )
    return attended[None], gradient[None], reward[0, :1]


def solution(mesh):
    return jax.shard_map(
        functools.partial(on_device, mesh.shape["dp"], mesh.shape["seq"]),
        mesh=mesh,
        in_specs=(
            P("dp", "seq", None),
            P("dp", "seq", None),
            P("dp", "seq", None),
            P("dp", "seq", None),
            P("dp", "seq", None),
            P(),
            P(),
            P(),
            P(),
            P(),
            P(),
            P(("dp", "seq"), None),
            P(("dp", "seq"), None),
            P(),
        ),
        out_specs=(P("dp", None, "seq"), P("dp", None, "seq"), P("dp")),
        check_vma=False,
    )
```

time: 220 us -> 84.1 us (0.38)
  waiting for transfers between devices: 76.2 us -> 0 us
  Pallas kernels: 0 us -> 67.7 us
  other arithmetic: 52 us -> 0 us
  starting transfers between devices: 26.9 us -> 0 us
  between operations: 16.7 us -> 0.65 us
  matrix products: 15.7 us -> 0 us
  blocking collectives: 13.9 us -> 0 us
    pallas_call x0 -> x1, Pallas kernels: none -> 67.7 us  [on_device(): pl.pallas_call(functools.partial(tower_kernel, n_dp, n_seq, gather_here),...]
    psum x2 -> x0, waiting for transfers between devices: 67 us -> none  [the longest x1 33.7 us: on_device(): lax.psum(round_term(branch).astype(jnp.bfloat16), 'seq').astype(jnp.float32)]
    unnamed x5 -> x0, other arithmetic: 44.1 us -> none
    all_to_all x5 -> x0, starting transfers between devices: 26.8 us -> none  [the longest x1 6.32 us: on_device(): lax.all_to_all(image_query, 'seq', split_axis=2, concat_axis=1, tiled=True)]
    dot_general x7 -> x0, matrix products: 15.7 us -> none  [the longest x2 4.19 us: contract_rows(): lax.dot_general(left_side, right_side, (((1,), (1,)), ((), ())), preferre...]
    all_gather x1 -> x0, blocking collectives: 13.9 us -> none  [on_device(): lax.all_gather(pooled, 'seq', axis=1, tiled=True)]
    all_to_all x5 -> x0, waiting for transfers between devices: 7.74 us -> none  [the longest x1 7.72 us: on_device(): lax.all_to_all(text_value, 'seq', split_axis=2, concat_axis=1, tiled=True)]
    reduce_sum x9 -> x0, other arithmetic: 6.65 us -> none  [the longest x2 1.75 us: layer_back(): jnp.mean(upstream, axis=-1, keepdims=True)]
  transfers between devices with their start and end apart: 9 -> 0, of which waited for: 3 -> 0; matrix products, arithmetic and copies ran while one was open for 32% -> 0% of each run, Pallas kernels for 0% -> 0%
where the time goes in v1:
time: 84.1 us; the launch traced here: 83.5 us
  Pallas kernels  67.7 us (80%)
  local copies, waits for them, and re-layouts  15.2 us (18%)
    pallas_call x1, Pallas kernels, on_device(): pl.pallas_call(functools.partial(tower_kernel, n_dp, n_seq, gather_here),...  67.7 us
    unnamed x24, local copies, waits for them, and re-layouts  12.5 us

profile of v1, /device:TPU:0, one launch (start us, length us, event | category | flops | bytes accessed | tf_op | source)
XLA Modules:
  0.0 83.5 jit_solution(14483932259921346920)
XLA Ops:
  0.6 0.7 reshape.23.norm_gain_ref
  1.3 0.7 reshape.24.final_gain_ref
  2.0 0.7 reshape.25.direction_ref
  2.7 0.0 copy-start
  2.7 2.2 %copy-done = bf16[1536,1408]{1,0:T(8,128)(2,1)S(1)} copy-done((bf16[1536,1408]{1,0:T(8,128)(2,1)S(1)}, bf16[1536,1408]{1,0:T(8,128)(2,1)}, u32[]{:S(2)}) %copy-start) | copy-done | bytes 4325400
  5.0 0.0 copy-start.1
  5.0 1.0 %copy-done.1 = bf16[1,128,1536]{2,1,0:T(8,128)(2,1)S(1)} copy-done((bf16[1,128,1536]{2,1,0:T(8,128)(2,1)S(1)}, bf16[1,128,1536]{2,1,0:T(8,128)(2,1)}, u32[]{:S(2)}) %copy-start.1) | copy-done | bytes 393240
  6.0 1.0 %copy-done.2 = bf16[1,128,1536]{2,1,0:T(8,128)(2,1)S(1)} copy-done((bf16[1,128,1536]{2,1,0:T(8,128)(2,1)S(1)}, bf16[1,128,1536]{2,1,0:T(8,128)(2,1)}, u32[]{:S(2)}) %copy-start.2) | copy-done | bytes 393240
  7.0 0.0 copy-start.3
  7.0 1.0 %copy-done.3 = f32[64,1408]{1,0:T(8,128)S(1)} copy-done((f32[64,1408]{1,0:T(8,128)S(1)}, f32[64,1408]{1,0:T(8,128)}, u32[]{:S(2)}) %copy-start.3) | copy-done | bytes 360472
  7.9 0.0 copy-start.4
  7.9 1.0 %copy-done.4 = bf16[96,1408]{1,0:T(8,128)(2,1)S(1)} copy-done((bf16[96,1408]{1,0:T(8,128)(2,1)S(1)}, bf16[96,1408]{1,0:T(8,128)(2,1)}, u32[]{:S(2)}) %copy-start.4) | copy-done | bytes 270360
  8.9 0.0 copy-start.5
  8.9 1.0 %copy-done.5 = bf16[96,1408]{1,0:T(8,128)(2,1)S(1)} copy-done((bf16[96,1408]{1,0:T(8,128)(2,1)S(1)}, bf16[96,1408]{1,0:T(8,128)(2,1)}, u32[]{:S(2)}) %copy-start.5) | copy-done | bytes 270360
  9.8 0.0 copy-start.6
  9.8 0.9 %copy-done.6 = bf16[1,64,1536]{2,1,0:T(8,128)(2,1)S(1)} copy-done((bf16[1,64,1536]{2,1,0:T(8,128)(2,1)S(1)}, bf16[1,64,1536]{2,1,0:T(8,128)(2,1)}, u32[]{:S(2)}) %copy-start.6) | copy-done | bytes 196632
  10.8 0.9 %copy-done.7 = bf16[1,64,1536]{2,1,0:T(8,128)(2,1)S(1)} copy-done((bf16[1,64,1536]{2,1,0:T(8,128)(2,1)S(1)}, bf16[1,64,1536]{2,1,0:T(8,128)(2,1)}, u32[]{:S(2)}) %copy-start.7) | copy-done | bytes 196632
  11.7 0.9 %copy-done.8 = bf16[1,64,1536]{2,1,0:T(8,128)(2,1)S(1)} copy-done((bf16[1,64,1536]{2,1,0:T(8,128)(2,1)S(1)}, bf16[1,64,1536]{2,1,0:T(8,128)(2,1)}, u32[]{:S(2)}) %copy-start.8) | copy-done | bytes 196632
  12.6 0.7 copy-done.9
  13.3 0.7 copy-done.10
  13.9 67.7 %shard_map.157 = (bf16[256,384]{1,0:T(8,128)(2,1)S(1)}, bf16[256,384]{1,0:T(8,128)(2,1)S(1)}, f32[8,128]{1,0:T(8,128)S(1)}) custom-call(bf16[1,64,1536]{2,1,0:T(8,128)(2,1)S(1)} %copy-done.6, bf16[1,64,1536]{2,1,0:T(8,128)(2,1)S(1)} %copy-done.7, bf16[1,64,1536]{2,1,0:T(8,128)(2,1)S(1)} %copy-done.8, bf16[1,128,1536]{2,1,0:T(8,128)(2,1)S(1)} %copy-done.1, ...), custom_call_target="tpu_custom_call" | custom-call | tf_op jit(solution)/shard_map/pallas_call | solution.py:399
  81.7 0.5 slice.3
  82.2 0.7 copy.19
  82.9 0.7 copy.20
  (5 shorter events, 0.0 us)
Async XLA Ops:
  2.7 2.2 %copy-start = (bf16[1536,1408]{1,0:T(8,128)(2,1)S(1)}, bf16[1536,1408]{1,0:T(8,128)(2,1)}, u32[]{:S(2)}) copy-start(bf16[1536,1408]{1,0:T(8,128)(2,1)} %embed_hbm.1) | copy-start | bytes 12976132
  5.0 1.0 %copy-start.1 = (bf16[1,128,1536]{2,1,0:T(8,128)(2,1)S(1)}, bf16[1,128,1536]{2,1,0:T(8,128)(2,1)}, u32[]{:S(2)}) copy-start(bf16[1,128,1536]{2,1,0:T(8,128)(2,1)} %tk_ref.1) | copy-start | bytes 1179652
  6.0 1.0 %copy-start.2 = (bf16[1,128,1536]{2,1,0:T(8,128)(2,1)S(1)}, bf16[1,128,1536]{2,1,0:T(8,128)(2,1)}, u32[]{:S(2)}) copy-start(bf16[1,128,1536]{2,1,0:T(8,128)(2,1)} %tv_ref.1) | copy-start | bytes 1179652
  7.0 1.0 %copy-start.3 = (f32[64,1408]{1,0:T(8,128)S(1)}, f32[64,1408]{1,0:T(8,128)}, u32[]{:S(2)}) copy-start(f32[64,1408]{1,0:T(8,128)} %pos_ref.1) | copy-start | bytes 1081348
  7.9 1.0 %copy-start.4 = (bf16[96,1408]{1,0:T(8,128)(2,1)S(1)}, bf16[96,1408]{1,0:T(8,128)(2,1)}, u32[]{:S(2)}) copy-start(bf16[96,1408]{1,0:T(8,128)(2,1)} %up_hbm.1) | copy-start | bytes 811012
  8.9 1.0 %copy-start.5 = (bf16[96,1408]{1,0:T(8,128)(2,1)S(1)}, bf16[96,1408]{1,0:T(8,128)(2,1)}, u32[]{:S(2)}) copy-start(bf16[96,1408]{1,0:T(8,128)(2,1)} %down_hbm.1) | copy-start | bytes 811012
  9.8 0.9 %copy-start.6 = (bf16[1,64,1536]{2,1,0:T(8,128)(2,1)S(1)}, bf16[1,64,1536]{2,1,0:T(8,128)(2,1)}, u32[]{:S(2)}) copy-start(bf16[1,64,1536]{2,1,0:T(8,128)(2,1)} %iq_ref.1) | copy-start | bytes 589828
  10.8 0.9 %copy-start.7 = (bf16[1,64,1536]{2,1,0:T(8,128)(2,1)S(1)}, bf16[1,64,1536]{2,1,0:T(8,128)(2,1)}, u32[]{:S(2)}) copy-start(bf16[1,64,1536]{2,1,0:T(8,128)(2,1)} %ik_ref.1) | copy-start | bytes 589828
  11.7 0.9 %copy-start.8 = (bf16[1,64,1536]{2,1,0:T(8,128)(2,1)S(1)}, bf16[1,64,1536]{2,1,0:T(8,128)(2,1)}, u32[]{:S(2)}) copy-start(bf16[1,64,1536]{2,1,0:T(8,128)(2,1)} %iv_ref.1) | copy-start | bytes 589828
  12.6 0.7 copy-start.9
  13.3 0.7 copy-start.10

commit v2 on v1

--- a/solution.py
+++ b/solution.py
@@ -49,6 +49,19 @@
 
 def dot_rows(left, right):
     return lax.dot_general(left, right, (((1,), (1,)), ((), ())), preferred_element_type=F32)
+
+
+def pool_map(shape, token_axis):
+    token = lax.broadcasted_iota(jnp.int32, shape, token_axis)
+    pool = lax.broadcasted_iota(jnp.int32, shape, 1 - token_axis)
+    place = lax.div(token, 2 * PATCH_W) * (PATCH_W // 2) + lax.div(lax.rem(token, PATCH_W), 2)
+    return jnp.where(place == pool, 0.25, 0.0).astype(BF16)
+
+
+def finish_kernel(attended_ref, slope_ref, attended_out, gradient_ref):
+    attended_out[...] = attended_ref[...]
+    shape = (gradient_ref.shape[0], slope_ref.shape[0])
+    gradient_ref[...] = dot(pool_map(shape, 0), slope_ref[...]).astype(BF16)
 
 
 def tower_kernel(
@@ -60,21 +73,27 @@
     iv_ref,
     tk_ref,
     tv_ref,
-    q_gain_ref,
-    k_gain_ref,
+    q_gain_hbm,
+    k_gain_hbm,
     embed_hbm,
-    pos_ref,
-    norm_gain_ref,
-    final_gain_ref,
+    pos_hbm,
+    norm_gain_hbm,
+    final_gain_hbm,
     up_hbm,
     down_hbm,
-    direction_ref,
+    direction_hbm,
     attended_ref,
-    gradient_ref,
+    slope_ref,
     reward_ref,
     q_buf,
     k_buf,
     v_buf,
+    q_gain_ref,
+    k_gain_ref,
+    pos_ref,
+    norm_gain_ref,
+    final_gain_ref,
+    direction_ref,
     embed,
     up_all,
     down_all,
@@ -85,7 +104,8 @@
     slope_all,
     part2_buf,
     part2_in,
-    slope2_all,
+    slope2_out,
+    slope2_in,
     score_buf,
     local_sem,
     a2a_send,
@@ -145,11 +165,17 @@
     own_loads = []
     for index, (src, dst) in enumerate(pieces(seq, 0)):
         own_loads.append(pltpu.make_async_copy(src, dst, local_sem.at[index]))
+    for index, (src, dst) in enumerate(((q_gain_hbm, q_gain_ref), (k_gain_hbm, k_gain_ref))):
+        own_loads.append(pltpu.make_async_copy(src, dst, local_sem.at[8 + index]))
     own_rows = rows(dp, shard) if gather_here else pl.ds(0, shard)
     late_loads = [
         pltpu.make_async_copy(embed_hbm, embed, local_sem.at[5]),
         pltpu.make_async_copy(up_hbm, up_all.at[own_rows], local_sem.at[6]),
         pltpu.make_async_copy(down_hbm, down_all.at[own_rows], local_sem.at[7]),
+        pltpu.make_async_copy(pos_hbm, pos_ref, local_sem.at[10]),
+        pltpu.make_async_copy(norm_gain_hbm, norm_gain_ref, local_sem.at[11]),
+        pltpu.make_async_copy(final_gain_hbm, final_gain_ref, local_sem.at[12]),
+        pltpu.make_async_copy(direction_hbm, direction_ref, local_sem.at[13]),
     ]
     for load in own_loads:
         load.start()
@@ -213,8 +239,8 @@
     for d in range(1, n_seq):
         a2a[d, 0].wait_recv()
 
-    q_gain = q_gain_ref[...]
-    k_gain = k_gain_ref[...]
+    q_gain = q_gain_ref[...].reshape(1, -1)
+    k_gain = k_gain_ref[...].reshape(1, -1)
     queries = []
     for h in range(heads):
         lanes = slice(h * HEAD, (h + 1) * HEAD)
@@ -241,12 +267,6 @@
         for d in range(n_seq):
             attended_ref[rows(source(d), img), lanes] = done[d * img : (d + 1) * img]
 
-    def pool_map(shape, token_axis):
-        token = lax.broadcasted_iota(jnp.int32, shape, token_axis)
-        pool = lax.broadcasted_iota(jnp.int32, shape, 1 - token_axis)
-        place = lax.div(token, 2 * PATCH_W) * (PATCH_W // 2) + lax.div(lax.rem(token, PATCH_W), 2)
-        return jnp.where(place == pool, 0.25, 0.0).astype(BF16)
-
     image_tokens = attended_ref.shape[0]
     pooled = dot(pool_map((tokens, image_tokens), 1), attended_ref[...])
     pooled_buf[0] = pooled.astype(BF16)
@@ -281,7 +301,7 @@
         residual = residual + dot(pooled_buf[d], embed[rows(source(d), width), :])
     resid_in[...] = residual
     normed_in, _ = layer_stats(residual)
-    norm_gain = norm_gain_ref[...]
+    norm_gain = norm_gain_ref[...].reshape(1, -1)
     hidden_in = (normed_in * norm_gain).astype(BF16)
     if gather_here:
         for d in range(n_chip):
@@ -301,7 +321,7 @@
         part_copies[d].wait_recv()
         branch = branch + part_in[d].astype(F32)
     normed_out, inverse_out = layer_stats(own_resid + branch)
-    direction = final_gain_ref[...] * direction_ref[...]
+    direction = (final_gain_ref[...] * direction_ref[...]).reshape(1, -1)
     out_slope = layer_back(direction, normed_out, inverse_out)
     slope_all[rows(seq, mine), :] = out_slope.astype(BF16)
     own_tokens = rows(seq, mine)
@@ -334,19 +354,21 @@
         part2_copies[d].wait_recv()
         slope_in = slope_in + part2_in[d].astype(F32)
     input_slope = out_slope + layer_back(slope_in * norm_gain, normed_own, inverse_own)
-    slope2_all[rows(seq, mine), :] = input_slope.astype(BF16)
+    pooled_own = dot_rows(input_slope.astype(BF16), embed[...]).astype(BF16)
+    for owner in range(n_seq):
+        slope2_out[owner] = pooled_own[:, owner * width : (owner + 1) * width]
+    slope2_in[rows(seq, mine), :] = slope2_out[seq]
     slope2_copies = spread_to(
-        4, lambda d: slope2_all.at[own_tokens], lambda d: slope2_all.at[own_tokens]
+        4, lambda d: slope2_out.at[peer(d)], lambda d: slope2_in.at[own_tokens]
     )
     score_sum = score_buf[0]
     for d in range(1, n_seq):
         score_copies[d].wait_recv()
         score_sum = score_sum + score_buf[d]
-    reward_ref[...] = score_sum * (1.0 / tokens)
+    reward_ref[0] = score_sum[0, 0] * (1.0 / tokens)
     for d in range(1, n_seq):
         slope2_copies[d].wait_recv()
-    pooled_slope = dot_rows(slope2_all[...], embed[rows(seq, width), :]).astype(BF16)
-    gradient_ref[...] = dot(pool_map((image_tokens, tokens), 0), pooled_slope).astype(BF16)
+    slope_ref[...] = slope2_in[...]
 
     for group in (
         a2a,
@@ -394,26 +416,26 @@
     n_chip = n_dp // 2 if gather_here else 1
     keys = img + txt
     vmem = pl.BlockSpec(memory_space=pltpu.VMEM)
-    anywhere = pl.BlockSpec(memory_space=pl.ANY)
     dma = pltpu.SemaphoreType.DMA
-    attended, gradient, reward = pl.pallas_call(
+    attended, slope, reward = pl.pallas_call(
         functools.partial(tower_kernel, n_dp, n_seq, gather_here),
         out_shape=(
             jax.ShapeDtypeStruct((img * n_seq, width), BF16),
-            jax.ShapeDtypeStruct((img * n_seq, width), BF16),
-            jax.ShapeDtypeStruct((8, 128), F32),
+            jax.ShapeDtypeStruct((tokens, width), BF16),
+            jax.ShapeDtypeStruct((1,), F32),
         ),
-        in_specs=[anywhere] * 5
-        + [vmem] * 2
-        + [anywhere]
-        + [vmem] * 3
-        + [anywhere] * 2
-        + [vmem],
-        out_specs=(vmem, vmem, vmem),
+        in_specs=[pl.BlockSpec(memory_space=pltpu.HBM)] * 14,
+        out_specs=(vmem, vmem, pl.BlockSpec(memory_space=pltpu.SMEM)),
         scratch_shapes=[
             pltpu.VMEM((n_seq, img, width), BF16),
             pltpu.VMEM((n_seq, keys, width), BF16),
             pltpu.VMEM((n_seq, keys, width), BF16),
+            pltpu.VMEM((HEAD,), F32),
+            pltpu.VMEM((HEAD,), F32),
+            pltpu.VMEM((tokens, emb), F32),
+            pltpu.VMEM((emb,), F32),
+            pltpu.VMEM((emb,), F32),
+            pltpu.VMEM((emb,), F32),
             pltpu.VMEM((features, emb), BF16),
             pltpu.VMEM((hidden, emb), BF16),
             pltpu.VMEM((hidden, emb), BF16),
@@ -424,9 +446,10 @@
             pltpu.VMEM((tokens, emb), BF16),
             pltpu.VMEM((tokens, emb), BF16),
             pltpu.VMEM((n_seq, mine, emb), BF16),
-            pltpu.VMEM((tokens, emb), BF16),
+            pltpu.VMEM((n_seq, mine, width), BF16),
+            pltpu.VMEM((tokens, width), BF16),
             pltpu.VMEM((n_seq, 8, 128), F32),
-            dma((8,)),
+            dma((14,)),
             dma((n_seq, 5)),
             dma((n_seq, 5)),
             dma((n_chip, 2)),
@@ -439,7 +462,7 @@
             dma((n_seq,)),
         ],
         compiler_params=pltpu.CompilerParams(
-            collective_id=0, has_side_effects=True, vmem_limit_bytes=40 * 1024 * 1024
+            collective_id=0, has_side_effects=True, vmem_limit_bytes=(64 * 1024 - 256) * 1024
         ),
     )(
         image_query,
@@ -447,17 +470,24 @@
         image_value,
         text_key,
         text_value,
-        query_gain.reshape(1, -1),
-        key_gain.reshape(1, -1),
+        query_gain,
+        key_gain,
         embed_weight,
         position_embed,
-        norm_gain.reshape(1, -1),
-        final_gain.reshape(1, -1),
+        norm_gain,
+        final_gain,
         up_weight,
         down_weight,
-        reward_direction.reshape(1, -1),
-    )
-    return attended[None], gradient[None], reward[0, :1]
+        reward_direction,
+    )
+    result = jax.ShapeDtypeStruct((img * n_seq, width), BF16)
+    attended, gradient = pl.pallas_call(
+        finish_kernel,
+        out_shape=(result, result),
+        in_specs=[vmem, vmem],
+        out_specs=(vmem, vmem),
+    )(attended, slope)
+    return attended[None], gradient[None], reward
 
 
 def solution(mesh):

time: 84.1 us -> 71.7 us (0.85)
  local copies, waits for them, and re-layouts: 15.2 us -> 0 us
  between operations: 0.65 us -> 2.41 us
  Pallas kernels: 67.7 us -> 69.1 us
    unnamed x24 -> x0, local copies, waits for them, and re-layouts: 12.5 us -> none
    reshape x3 -> x0, local copies, waits for them, and re-layouts: 2.1 us -> none  [the longest x1 0.7 us: on_device(): norm_gain.reshape(1, -1)]
    pallas_call x0 -> x1, Pallas kernels: none -> 1.8 us  [on_device(): pl.pallas_call(finish_kernel, out_shape=(result, result), in_specs=[vmem,...]
where the time goes in v2:
time: 71.7 us; the launch traced here: 71.5 us
  Pallas kernels  69.1 us (96%)
  between operations  2.41 us (3%)
    pallas_call x1, Pallas kernels, on_device(): pl.pallas_call(functools.partial(tower_kernel, n_dp, n_seq, gather_here),...  67.3 us
    pallas_call x1, Pallas kernels, on_device(): pl.pallas_call(finish_kernel, out_shape=(result, result), in_specs=[vmem,...  1.8 us

profile of v2, /device:TPU:0, one launch (start us, length us, event | category | flops | bytes accessed | tf_op | source)
XLA Modules:
  0.0 71.5 jit_solution(9551838038656439136)
XLA Ops:
  0.6 67.3 %shard_map.157 = (bf16[256,384]{1,0:T(8,128)(2,1)}, bf16[64,384]{1,0:T(8,128)(2,1)}, f32[1]{0:T(128)}) custom-call(bf16[1,64,1536]{2,1,0:T(8,128)(2,1)} %iq_ref.1, bf16[1,64,1536]{2,1,0:T(8,128)(2,1)} %ik_ref.1, bf16[1,64,1536]{2,1,0:T(8,128)(2,1)} %iv_ref.1, bf16[1,128,1536]{2,1,0:T(8,128)(2,1)} %tk_ref.1, bf16[1,128,1536]{2,1,0:T(8,128)(2,1)} %tv_ref.1, ...), custom_call_target="tpu_custom_call" | custom-call | tf_op jit(solution)/shard_map/pallas_call | solution.py:420
  68.0 1.8 %shard_map.158 = (bf16[256,384]{1,0:T(8,128)(2,1)}, bf16[256,384]{1,0:T(8,128)(2,1)}) custom-call(bf16[256,384]{1,0:T(8,128)(2,1)} %get-tuple-element.8.attended_ref, bf16[64,384]{1,0:T(8,128)(2,1)} %get-tuple-element.9.slope_ref), custom_call_target="tpu_custom_call" | custom-call | tf_op jit(solution)/shard_map/pallas_call | solution.py:484

commit v3 on v2

--- a/solution.py
+++ b/solution.py
@@ -88,6 +88,10 @@
     q_buf,
     k_buf,
     v_buf,
+    mix_out,
+    mix_in,
+    total_out,
+    total_in,
     q_gain_ref,
     k_gain_ref,
     pos_ref,
@@ -108,8 +112,12 @@
     slope2_in,
     score_buf,
     local_sem,
-    a2a_send,
-    a2a_recv,
+    q_send,
+    q_recv,
+    kv_send,
+    kv_recv,
+    mix_send,
+    mix_recv,
     w_send,
     w_recv,
     f_send,
@@ -121,7 +129,7 @@
 ):
     dp = lax.axis_index("dp")
     seq = lax.axis_index("seq")
-    width = q_buf.shape[2]
+    width = q_buf.shape[3]
     heads = width // HEAD
     img = iq_ref.shape[1]
     txt = tk_ref.shape[1]
@@ -129,6 +137,9 @@
     tokens = resid_in.shape[0]
     mine = tokens // n_seq
     n_chip = n_dp // 2
+    half = n_seq // 2
+    place = lax.rem(seq, half)
+    base = seq - place
     core = lax.rem(dp, 2)
     chip = lax.div(dp, 2)
 
@@ -152,19 +163,26 @@
     def rows(owner, count):
         return pl.ds(pl.multiple_of(owner * count, 16), count)
 
-    def pieces(owner, slot):
-        cols = columns(owner)
+    def group(owner, which):
+        return columns(owner if which else lax.rem(owner + half, n_seq))
+
+    def query_piece(owner, which):
+        return iq_ref.at[0, :, group(owner, which)], q_buf.at[seq, which]
+
+    def key_pieces(owner, which, slot):
+        cols = group(owner, which)
         return (
-            (iq_ref.at[0, :, cols], q_buf.at[slot]),
-            (tk_ref.at[0, :, cols], k_buf.at[slot, pl.ds(0, txt)]),
-            (ik_ref.at[0, :, cols], k_buf.at[slot, pl.ds(txt, img)]),
-            (tv_ref.at[0, :, cols], v_buf.at[slot, pl.ds(0, txt)]),
-            (iv_ref.at[0, :, cols], v_buf.at[slot, pl.ds(txt, img)]),
+            (tk_ref.at[0, :, cols], k_buf.at[slot, which, pl.ds(0, txt)]),
+            (ik_ref.at[0, :, cols], k_buf.at[slot, which, pl.ds(txt, img)]),
+            (tv_ref.at[0, :, cols], v_buf.at[slot, which, pl.ds(0, txt)]),
+            (iv_ref.at[0, :, cols], v_buf.at[slot, which, pl.ds(txt, img)]),
         )
 
     own_loads = []
-    for index, (src, dst) in enumerate(pieces(seq, 0)):
-        own_loads.append(pltpu.make_async_copy(src, dst, local_sem.at[index]))
+    for which in range(2):
+        for src, dst in (query_piece(seq, which), *key_pieces(seq, which, 0)):
+            index = 14 + len(own_loads)
+            own_loads.append(pltpu.make_async_copy(src, dst, local_sem.at[index]))
     for index, (src, dst) in enumerate(((q_gain_hbm, q_gain_ref), (k_gain_hbm, k_gain_ref))):
         own_loads.append(pltpu.make_async_copy(src, dst, local_sem.at[8 + index]))
     own_rows = rows(dp, shard) if gather_here else pl.ds(0, shard)
@@ -194,19 +212,30 @@
     pl.semaphore_wait(barrier, partners)
 
     a2a = {}
-    for d in range(1, n_seq):
-        for index, (src, dst) in enumerate(pieces(peer(d), d)):
-            a2a[d, index] = pltpu.make_async_remote_copy(
+    for which in range(2):
+        for d in range(1, n_seq):
+            src, dst = query_piece(peer(d), which)
+            a2a[d, which] = pltpu.make_async_remote_copy(
                 src_ref=src,
                 dst_ref=dst,
-                send_sem=a2a_send.at[d, index],
-                recv_sem=a2a_recv.at[d, index],
+                send_sem=q_send.at[d, which],
+                recv_sem=q_recv.at[d, which],
                 device_id=(dp, peer(d)),
                 device_id_type=MESH,
             )
-    for index in range(5):
-        for d in range(1, n_seq):
-            a2a[d, index].start()
+            a2a[d, which].start()
+        for e in range(1, half):
+            target = base + lax.rem(place + e, half)
+            for index, (src, dst) in enumerate(key_pieces(target, which, e)):
+                a2a[e, which, index] = pltpu.make_async_remote_copy(
+                    src_ref=src,
+                    dst_ref=dst,
+                    send_sem=kv_send.at[e, which, index],
+                    recv_sem=kv_recv.at[e, which, index],
+                    device_id=(dp, target),
+                    device_id_type=MESH,
+                )
+                a2a[e, which, index].start()
 
     weights, forwards = {}, {}
     if gather_here:
@@ -236,36 +265,57 @@
         load.start()
     for load in own_loads:
         load.wait()
-    for d in range(1, n_seq):
-        a2a[d, 0].wait_recv()
 
     q_gain = q_gain_ref[...].reshape(1, -1)
     k_gain = k_gain_ref[...].reshape(1, -1)
-    queries = []
+    ones = jnp.ones((total_out.shape[1], txt + img), BF16)
+    mix_copies = {}
+    for which in range(2):
+        for d in range(1, n_seq):
+            a2a[d, which].wait_recv()
+        mixed = [None] * heads
+        total = [None] * heads
+        queries = []
+        for h in range(heads):
+            lanes = slice(h * HEAD, (h + 1) * HEAD)
+            parts = [norm_head(q_buf[j, which, :, lanes], q_gain) for j in range(n_seq)]
+            queries.append(jnp.concatenate(parts, axis=0))
+        for e in range(half):
+            if e:
+                for index in range(4):
+                    a2a[e, which, index].wait_recv()
+            for h in range(heads):
+                lanes = slice(h * HEAD, (h + 1) * HEAD)
+                keys = norm_head(k_buf[e, which, :, lanes], k_gain)
+                exponent = jnp.exp(dot_rows(queries[h], keys) * HEAD**-0.5)
+                narrow = exponent.astype(BF16)
+                if which:
+                    part_total = jnp.sum(exponent, axis=-1, keepdims=True)
+                else:
+                    part_total = dot_rows(ones, narrow)
+                part_mixed = dot(narrow, v_buf[e, which, :, lanes])
+                total[h] = part_total if e == 0 else total[h] + part_total
+                mixed[h] = part_mixed if e == 0 else mixed[h] + part_mixed
+        if not which:
+            for h in range(heads):
+                mix_out[:, h * HEAD : (h + 1) * HEAD] = mixed[h].astype(BF16)
+                total_out[h] = total[h]
+            for index, (src, dst) in enumerate(((mix_out, mix_in), (total_out, total_in))):
+                mix_copies[index] = pltpu.make_async_remote_copy(
+                    src_ref=src,
+                    dst_ref=dst,
+                    send_sem=mix_send.at[index],
+                    recv_sem=mix_recv.at[index],
+                    device_id=(dp, peer(half)),
+                    device_id_type=MESH,
+                )
+                mix_copies[index].start()
+    for index in range(2):
+        mix_copies[index].wait_recv()
     for h in range(heads):
         lanes = slice(h * HEAD, (h + 1) * HEAD)
-        queries.append(
-            jnp.concatenate([norm_head(q_buf[d, :, lanes], q_gain) for d in range(n_seq)], axis=0)
-        )
-    mixed = [None] * heads
-    total = [None] * heads
-    for d in range(n_seq):
-        if d:
-            for index in range(1, 5):
-                a2a[d, index].wait_recv()
-        for h in range(heads):
-            lanes = slice(h * HEAD, (h + 1) * HEAD)
-            keys = norm_head(k_buf[d, :, lanes], k_gain)
-            exponent = jnp.exp(dot_rows(queries[h], keys) * HEAD**-0.5)
-            part_total = jnp.sum(exponent, axis=-1, keepdims=True)
-            part_mixed = dot(exponent.astype(BF16), v_buf[d, :, lanes])
-            total[h] = part_total if d == 0 else total[h] + part_total
-            mixed[h] = part_mixed if d == 0 else mixed[h] + part_mixed
-    for h in range(heads):
-        lanes = slice(h * HEAD, (h + 1) * HEAD)
-        done = (mixed[h] / total[h]).astype(BF16)
-        for d in range(n_seq):
-            attended_ref[rows(source(d), img), lanes] = done[d * img : (d + 1) * img]
+        whole = total[h] + jnp.transpose(total_in[h])[:, 0:1]
+        attended_ref[:, lanes] = ((mixed[h] + mix_in[:, lanes].astype(F32)) / whole).astype(BF16)
 
     image_tokens = attended_ref.shape[0]
     pooled = dot(pool_map((tokens, image_tokens), 1), attended_ref[...])
@@ -372,6 +422,7 @@
 
     for group in (
         a2a,
+        mix_copies,
         weights,
         forwards,
         pooled_copies,
@@ -427,9 +478,13 @@
         in_specs=[pl.BlockSpec(memory_space=pltpu.HBM)] * 14,
         out_specs=(vmem, vmem, pl.BlockSpec(memory_space=pltpu.SMEM)),
         scratch_shapes=[
-            pltpu.VMEM((n_seq, img, width), BF16),
-            pltpu.VMEM((n_seq, keys, width), BF16),
-            pltpu.VMEM((n_seq, keys, width), BF16),
+            pltpu.VMEM((n_seq, 2, img, width), BF16),
+            pltpu.VMEM((n_seq // 2, 2, keys, width), BF16),
+            pltpu.VMEM((n_seq // 2, 2, keys, width), BF16),
+            pltpu.VMEM((n_seq * img, width), BF16),
+            pltpu.VMEM((n_seq * img, width), BF16),
+            pltpu.VMEM((width // HEAD, 8, n_seq * img), F32),
+            pltpu.VMEM((width // HEAD, 8, n_seq * img), F32),
             pltpu.VMEM((HEAD,), F32),
             pltpu.VMEM((HEAD,), F32),
             pltpu.VMEM((tokens, emb), F32),
@@ -449,9 +504,13 @@
             pltpu.VMEM((n_seq, mine, width), BF16),
             pltpu.VMEM((tokens, width), BF16),
             pltpu.VMEM((n_seq, 8, 128), F32),
-            dma((14,)),
-            dma((n_seq, 5)),
-            dma((n_seq, 5)),
+            dma((24,)),
+            dma((n_seq, 2)),
+            dma((n_seq, 2)),
+            dma((n_seq // 2, 2, 4)),
+            dma((n_seq // 2, 2, 4)),
+            dma((2,)),
+            dma((2,)),
             dma((n_chip, 2)),
             dma((n_chip, 2)),
             dma((n_chip, 2)),

time: 71.7 us -> 67.4 us (0.940)
  Pallas kernels: 69.1 us -> 64.8 us
    pallas_call x1, Pallas kernels: 67.3 us -> 63 us  [on_device(): pl.pallas_call(functools.partial(tower_kernel, n_dp, n_seq, gather_here),...]
where the time goes in v3:
time: 67.4 us; the launch traced here: 67.2 us
  Pallas kernels  64.8 us (96%)
  between operations  2.41 us (4%)
    pallas_call x1, Pallas kernels, on_device(): pl.pallas_call(functools.partial(tower_kernel, n_dp, n_seq, gather_here),...  63 us
    pallas_call x1, Pallas kernels, on_device(): pl.pallas_call(finish_kernel, out_shape=(result, result), in_specs=[vmem,...  1.8 us

profile of v3, /device:TPU:0, one launch (start us, length us, event | category | flops | bytes accessed | tf_op | source)
XLA Modules:
  0.0 67.2 jit_solution(4485148236845131956)
XLA Ops:
  0.6 63.0 %shard_map.157 = (bf16[256,384]{1,0:T(8,128)(2,1)}, bf16[64,384]{1,0:T(8,128)(2,1)}, f32[1]{0:T(128)}) custom-call(bf16[1,64,1536]{2,1,0:T(8,128)(2,1)} %iq_ref.1, bf16[1,64,1536]{2,1,0:T(8,128)(2,1)} %ik_ref.1, bf16[1,64,1536]{2,1,0:T(8,128)(2,1)} %iv_ref.1, bf16[1,128,1536]{2,1,0:T(8,128)(2,1)} %tk_ref.1, bf16[1,128,1536]{2,1,0:T(8,128)(2,1)} %tv_ref.1, ...), custom_call_target="tpu_custom_call" | custom-call | tf_op jit(solution)/shard_map/pallas_call | solution.py:471
  63.7 1.8 %shard_map.158 = (bf16[256,384]{1,0:T(8,128)(2,1)}, bf16[256,384]{1,0:T(8,128)(2,1)}) custom-call(bf16[256,384]{1,0:T(8,128)(2,1)} %get-tuple-element.8.attended_ref, bf16[64,384]{1,0:T(8,128)(2,1)} %get-tuple-element.9.slope_ref), custom_call_target="tpu_custom_call" | custom-call | tf_op jit(solution)/shard_map/pallas_call | solution.py:543
